TPU v7x, 32 devices: a whole 2x2x4 slice. The times are simulated.
32 devices in a mesh: chan: 8 (over z, y), band: 4 (over x, core).
Axes of the slice: x: 2, y: 2, z: 4, core: 2. Of those that a mesh axis runs over, the one named last changes fastest.
Arguments:
- traces: bfloat16 [2048, 2, 4096], P('chan', None, 'band')
- row_ids: int32 [2048], P('chan'), may hold values from 0 to 2047, as said below
Outputs:
- cross: float32 [2, 64, 5, 8, 4096], P(None, 'chan', None, None, 'band')
Inputs may be any that keep to these rules, and one draw needn't show every extreme that they name: Every channel-window number appears exactly once in row_ids. Of the rows held by one index of chan, at most 64 have row id // 256 equal to any one value, and that bound is reached.
All inputs are finite; a program needn't handle non-finite values.
Results may differ from a plain program's by a relative error of at most 0.003.
Values may be sent and summed in bfloat16 or wider, within the bound.
A program may use at most 64 MiB of HBM per device.

v0:
```python
import jax
import jax.numpy as jnp
from jax import lax
from jax.sharding import PartitionSpec as P

F = 4096
WIN = 32
H = 2


def passed_along(block, axis, distance):
    devices = range(lax.axis_size(axis))
    route = [(i - distance, i) for i in devices if i - distance in devices]
    return lax.ppermute(block, axis, route)


def row_power(trace_rows):
    values = trace_rows.astype(jnp.float32)
    return jnp.sum(values * values, axis=1)


def scale_rows(trace_rows, power_total):
    factor = 1.0 / jnp.sqrt(power_total / F + 1e-06)
    return (trace_rows.astype(jnp.float32) * factor[:, None]).astype(jnp.bfloat16)


def spectra_pair(first, second):
    first_real = first[:, None, :, 0].astype(jnp.float32)
    first_imag = first[:, None, :, 1].astype(jnp.float32)
    second_real = second[None, :, :, 0].astype(jnp.float32)
    second_imag = second[None, :, :, 1].astype(jnp.float32)
    real_part = jnp.sum(first_real * second_real + first_imag * second_imag, axis=2)
    imag_part = jnp.sum(first_imag * second_real - first_real * second_imag, axis=2)
    return jnp.stack([real_part, imag_part]) / WIN


def body(traces, row_ids):
    block_rows, _, band_bins = traces.shape
    trace_rows = traces.reshape(block_rows, 2 * band_bins)
    n_devices = lax.axis_size("chan")
    capacity = 2 * block_rows // n_devices
    trace_rows = scale_rows(trace_rows, lax.psum(row_power(trace_rows), "band"))
    owner_block = row_ids // block_rows
    member = (owner_block[:, None] == jnp.arange(n_devices)[None, :]).astype(jnp.int32)
    slot_rank = jnp.sum(member * (jnp.cumsum(member, axis=0) - 1), axis=1)
    slot_index = owner_block * capacity + slot_rank
    packing = slot_index[None, :] == jnp.arange(n_devices * capacity)[:, None]
    outgoing = jnp.dot(
        packing.astype(jnp.bfloat16), trace_rows, preferred_element_type=jnp.float32
    ).astype(jnp.bfloat16)
    label_values = (
        jnp.dot(
            packing.astype(jnp.float32),
            (row_ids + 1).astype(jnp.float32),
            precision=lax.Precision.HIGHEST,
        )
        - 1.0
    )
    sent_labels = label_values.astype(jnp.int32)
    arrived, arrived_ids = (
        lax.all_to_all(outgoing, "chan", split_axis=0, concat_axis=0, tiled=True),
        lax.all_to_all(sent_labels, "chan", split_axis=0, concat_axis=0, tiled=True),
    )
    placing = ((arrived_ids % block_rows)[None, :] == jnp.arange(block_rows)[:, None]) & (
        arrived_ids >= 0
    )[None, :]
    placed = jnp.dot(
        placing.astype(jnp.bfloat16), arrived, preferred_element_type=jnp.float32
    ).astype(jnp.bfloat16)
    chan_count = block_rows // WIN
    block_shape = (chan_count, WIN, 2, band_bins)
    local_block = placed.reshape(block_shape)
    spectra_list = [None] * (2 * H + 1)
    spectra_list[H] = spectra_pair(local_block, local_block)
    above_block = placed
    below_block = placed
    for offset in range(1, H + 1):
        above_block = passed_along(above_block, "chan", -1)
        spectra_list[H + offset] = spectra_pair(local_block, above_block.reshape(block_shape))
        below_block = passed_along(below_block, "chan", 1)
        spectra_list[H - offset] = spectra_pair(local_block, below_block.reshape(block_shape))
    return jnp.stack(spectra_list, axis=2)


def solution(mesh):
    in_specs = (P("chan", None, "band"), P("chan"))
    out_specs = P(None, "chan", None, None, "band")
    return jax.shard_map(body, mesh=mesh, in_specs=in_specs, out_specs=out_specs, check_vma=False)
```

profile of v0, /device:TPU:26, one launch (start us, length us, event | category | flops | bytes accessed | tf_op | source)
XLA Modules:
  0.0 209.3 jit_solution(1434791830120815046)
XLA Ops:
  0.0 0.7 add_convert_fusion.1
  0.7 0.6 reduce-window.6
  1.3 0.2 slice_reduce_fusion
  1.5 0.1 fusion.13
  1.6 0.3 fusion.6
  2.0 0.7 all_to_all.16
  2.7 6.1 %all-to-all-start = ((s32[8,64,1]{1,2,0:T(1,128)}), s32[8,64,1]{1,2,0:T(1,128)S(1)}, u32[]{:S(2)}, u32[]{:S(2)}) async-start(s32[8,64,1]{1,2,0:T(1,128)} %bitcast.5), calls=%async_computation | async-start | bytes 8192 | tf_op jit(solution)/shard_map/all_to_all | solution.py:62
  8.7 3.0 %multiply_reduce_fusion = f32[256]{0:T(256)S(1)} fusion(bf16[256,2,1024]{2,1,0:T(2,128)(2,1)} %param.2), kind=kLoop, calls=%fused_computation.13 | loop fusion | flops 1572608 | bytes 1049600 | tf_op jit(solution)/shard_map/reduce_sum | solution.py:19
  11.7 5.9 %psum.7 = f32[256]{0:T(256)S(1)} all-reduce(f32[256]{0:T(256)S(1)} %multiply_reduce_fusion), channel_id=1, replica_groups=mesh['chan'=8,'band'=4] {'band'}, use_global_device_ids=true, to_apply=%region_4.5 | all-reduce | flops 256 | bytes 2048 | tf_op jit(solution)/shard_map/psum | solution.py:42
  17.6 1.6 copy.16
  19.2 2.1 %convolution_convert_fusion = bf16[512,2048]{1,0:T(8,128)(2,1)} fusion(f32[256,2048]{1,0:T(8,128)S(1)} %bitcast.49, f32[256]{0:T(256)S(1)} %add_rsqrt_fusion, s32[256]{0:T(256)S(1)} %multiply_add_fusion), kind=kOutput, calls=%fused_computation.10 | convolution fusion | flops 539099136 | bytes 4196352 | tf_op jit(solution)/shard_map/dot_general | solution.py:48
  21.3 0.0 all-to-all-done
  21.3 6.0 %all-to-all-start.1 = ((bf16[8,64,2048]{2,1,0:T(8,128)(2,1)}), bf16[8,64,2048]{2,1,0:T(8,128)(2,1)S(1)}, u32[]{:S(2)}, u32[]{:S(2)}) async-start(bf16[8,64,2048]{2,1,0:T(8,128)(2,1)} %bitcast.6), calls=%async_computation.1 | async-start | bytes 4194304 | tf_op jit(solution)/shard_map/all_to_all | solution.py:61
  27.3 0.6 broadcast.134
  27.9 0.7 reduce.6
  28.6 0.1 all_to_all.18
  28.7 45.1 %all-to-all-done.1 = bf16[8,64,2048]{2,1,0:T(8,128)(2,1)S(1)} async-done(((bf16[8,64,2048]{2,1,0:T(8,128)(2,1)}), bf16[8,64,2048]{2,1,0:T(8,128)(2,1)S(1)}, u32[]{:S(2)}, u32[]{:S(2)}) %all-to-all-start.1) | async-done | bytes 2097184 | tf_op jit(solution)/shard_map/all_to_all | solution.py:61
  73.8 1.7 convolution_convert_fusion.1
  75.5 1.9 collective-permute-start.2
  77.4 4.9 %collective-permute-start = (bf16[256,2048]{1,0:T(8,128)(2,1)}, bf16[256,2048]{1,0:T(8,128)(2,1)}, u32[]{:S(2)}, u32[]{:S(2)}) collective-permute-start(bf16[256,2048]{1,0:T(8,128)(2,1)} %convolution_convert_fusion.1), channel_id=1, source_target_pairs={{0,4},{4,8},{8,12},{12,16},{16,20},{20,24},{24,28},{1,5},{5,9},{9,... | collective-permute-start | bytes 3145736 | tf_op jit(solution)/shard_map/ppermute | solution.py:14
  82.4 1.8 reshape.328
  84.2 1.9 slice_convert_fusion.9
  86.1 0.5 copy_bitcast_fusion.7
  86.6 38.6 %collective-permute-done.2 = bf16[256,2048]{1,0:T(8,128)(2,1)} collective-permute-done((bf16[256,2048]{1,0:T(8,128)(2,1)}, bf16[256,2048]{1,0:T(8,128)(2,1)}, u32[]{:S(2)}, u32[]{:S(2)}) %collective-permute-start.2) | collective-permute-done | bytes 1048608 | tf_op jit(solution)/shard_map/ppermute | solution.py:14
  125.3 1.8 reshape.331
  127.1 1.9 collective-permute-start.3
  129.0 1.9 slice_convert_fusion.3
  131.0 0.0 collective-permute-done
  131.0 5.1 %collective-permute-start.1 = (bf16[256,2048]{1,0:T(8,128)(2,1)}, bf16[256,2048]{1,0:T(8,128)(2,1)}, u32[]{:S(2)}, u32[]{:S(2)}) collective-permute-start(bf16[256,2048]{1,0:T(8,128)(2,1)} %collective-permute-done), channel_id=1, source_target_pairs={{0,4},{4,8},{8,12},{12,16},{16,20},{20,24},{24,28},{1,5},{5,9},{9,... | collective-permute-start | bytes 3145736 | tf_op jit(solution)/shard_map/ppermute | solution.py:14
  136.1 1.8 copy_bitcast_fusion.2
  137.9 1.8 reshape.330
  139.7 1.9 slice_convert_fusion.5
  141.7 1.8 copy_bitcast_fusion.4
  143.5 32.5 %collective-permute-done.3 = bf16[256,2048]{1,0:T(8,128)(2,1)} collective-permute-done((bf16[256,2048]{1,0:T(8,128)(2,1)}, bf16[256,2048]{1,0:T(8,128)(2,1)}, u32[]{:S(2)}, u32[]{:S(2)}) %collective-permute-start.3) | collective-permute-done | bytes 1048608 | tf_op jit(solution)/shard_map/ppermute | solution.py:14
  176.0 1.8 reshape.332
  177.8 3.3 %slice_convert_fusion.1 = (f32[8,32,1,1024]{3,2,1,0:T(1,128)}, f32[8,32,1,1024]{3,2,1,0:T(1,128)}) fusion(bf16[8,32,2,1024]{3,2,1,0:T(2,128)(2,1)S(1)} %reshape.332), kind=kLoop, calls=%fused_computation.15 | loop fusion | flops 524288 | bytes 3145728 | tf_op jit(solution)/shard_map/convert_element_type | solution.py:30
  181.1 0.0 collective-permute-done.1
  181.1 1.8 reshape.329
  183.0 0.0 copy-start
  183.0 1.9 slice_convert_fusion.8
  184.9 0.5 copy_bitcast_fusion
  185.5 0.5 copy_bitcast_fusion.6
  185.9 0.7 copy-done.2
  186.6 0.3 copy-done.3
  187.0 0.3 copy-done.4
  187.3 0.3 copy-done.5
  187.6 19.7 %add_reduce_fusion = (f32[8,8,1024]{2,1,0:T(8,128)S(1)}, f32[8,8,1024]{2,1,0:T(8,128)S(1)}, f32[8,8,1024]{2,1,0:T(8,128)S(1)}, f32[8,8,1024]{2,1,0:T(8,128)S(1)}...) fusion(f32[8,32,1024]{2,1,0:T(8,128)S(1)} %get-tuple-element.33, ...), kind=kLoop, calls=%fused_computation.1 | loop fusion | flops 83230720 | bytes 13107200 | tf_op jit(solution)/shard_map/reduce_sum | solution.py:32
  207.6 1.7 copy.5
  (20 shorter events, 0.3 us)
Async XLA Ops:
  2.7 18.7 %all-to-all-start = ((s32[8,64,1]{1,2,0:T(1,128)}), s32[8,64,1]{1,2,0:T(1,128)S(1)}, u32[]{:S(2)}, u32[]{:S(2)}) async-start(s32[8,64,1]{1,2,0:T(1,128)} %bitcast.5), calls=%async_computation | async-start | bytes 8192 | tf_op jit(solution)/shard_map/all_to_all | solution.py:62
  21.3 52.5 %all-to-all-start.1 = ((bf16[8,64,2048]{2,1,0:T(8,128)(2,1)}), bf16[8,64,2048]{2,1,0:T(8,128)(2,1)S(1)}, u32[]{:S(2)}, u32[]{:S(2)}) async-start(bf16[8,64,2048]{2,1,0:T(8,128)(2,1)} %bitcast.6), calls=%async_computation.1 | async-start | bytes 4194304 | tf_op jit(solution)/shard_map/all_to_all | solution.py:61
  75.5 49.7 %collective-permute-start.2 = (bf16[256,2048]{1,0:T(8,128)(2,1)}, bf16[256,2048]{1,0:T(8,128)(2,1)}, u32[]{:S(2)}, u32[]{:S(2)}) collective-permute-start(bf16[256,2048]{1,0:T(8,128)(2,1)} %convolution_convert_fusion.1), channel_id=1, source_target_pairs={{4,0},{8,4},{12,8},{16,12},{20,16},{24,20},{28,24},{5,1},{9,5},{13... | collective-permute-start | bytes 3145736 | tf_op jit(solution)/shard_map/ppermute | solution.py:14
  77.4 53.5 %collective-permute-start = (bf16[256,2048]{1,0:T(8,128)(2,1)}, bf16[256,2048]{1,0:T(8,128)(2,1)}, u32[]{:S(2)}, u32[]{:S(2)}) collective-permute-start(bf16[256,2048]{1,0:T(8,128)(2,1)} %convolution_convert_fusion.1), channel_id=1, source_target_pairs={{0,4},{4,8},{8,12},{12,16},{16,20},{20,24},{24,28},{1,5},{5,9},{9,... | collective-permute-start | bytes 3145736 | tf_op jit(solution)/shard_map/ppermute | solution.py:14
  127.1 48.9 %collective-permute-start.3 = (bf16[256,2048]{1,0:T(8,128)(2,1)}, bf16[256,2048]{1,0:T(8,128)(2,1)}, u32[]{:S(2)}, u32[]{:S(2)}) collective-permute-start(bf16[256,2048]{1,0:T(8,128)(2,1)} %collective-permute-done.2), channel_id=1, source_target_pairs={{4,0},{8,4},{12,8},{16,12},{20,16},{24,20},{28,24},{5,1},{9,5},{13... | collective-permute-start | bytes 3145736 | tf_op jit(solution)/shard_map/ppermute | solution.py:14
  131.0 50.2 %collective-permute-start.1 = (bf16[256,2048]{1,0:T(8,128)(2,1)}, bf16[256,2048]{1,0:T(8,128)(2,1)}, u32[]{:S(2)}, u32[]{:S(2)}) collective-permute-start(bf16[256,2048]{1,0:T(8,128)(2,1)} %collective-permute-done), channel_id=1, source_target_pairs={{0,4},{4,8},{8,12},{12,16},{16,20},{20,24},{24,28},{1,5},{5,9},{9,... | collective-permute-start | bytes 3145736 | tf_op jit(solution)/shard_map/ppermute | solution.py:14
  183.0 2.0 copy-start
  183.0 2.0 copy-start.1
  185.4 1.2 copy-start.2
  185.4 1.5 copy-start.3
  185.4 1.8 copy-start.4
  185.4 2.1 %copy-start.5 = (f32[8,32,1024]{2,1,0:T(8,128)S(1)}, f32[8,32,1024]{2,1,0:T(8,128)}, u32[]{:S(2)}) copy-start(f32[8,32,1024]{2,1,0:T(8,128)} %get-tuple-element.38) | copy-start | bytes 3145732
where the time goes:
time: 210 us; the launch traced here: 209 us
  waiting for transfers between devices  116 us (55%)
  other arithmetic  36.1 us (17%)
  starting transfers between devices  25.9 us (12%)
  local copies, waits for them, and re-layouts  20.7 us (10%)
  blocking collectives  5.89 us (3%)
  matrix products  4.15 us (2%)
    ppermute x4, waiting for transfers between devices, passed_along(): return lax.ppermute(block, axis, route)  71.2 us
    all_to_all x1, waiting for transfers between devices, body(): lax.all_to_all(outgoing, 'chan', split_axis=0, concat_axis=0, tiled=True)  45.1 us
    reduce_sum x1, other arithmetic, spectra_pair(): jnp.sum(first_real * second_real + first_imag * second_imag, axis=2)  19.7 us
    ppermute x4, starting transfers between devices, passed_along(): return lax.ppermute(block, axis, route)  13.8 us
    convert_element_type x4, other arithmetic, spectra_pair(): second_real = second[None, :, :, 0].astype(jnp.float32)  9.06 us
    unnamed x18, local copies, waits for them, and re-layouts  8.29 us
    all_to_all x1, starting transfers between devices, body(): lax.all_to_all(sent_labels, 'chan', split_axis=0, concat_axis=0, tiled=True)  6.05 us
    all_to_all x1, starting transfers between devices, body(): lax.all_to_all(outgoing, 'chan', split_axis=0, concat_axis=0, tiled=True)  5.99 us
  transfers between devices with their start and end apart: 6, of which 3 were waited for; matrix products, arithmetic and copies ran while one was open for 14% of the time, Pallas kernels for 0%

commit v1 on v0

--- a/solution.py
+++ b/solution.py
@@ -1,6 +1,10 @@
+import functools
+
 import jax
 import jax.numpy as jnp
 from jax import lax
+from jax.experimental import pallas as pl
+from jax.experimental.pallas import tpu as pltpu
 from jax.sharding import PartitionSpec as P
 
 F = 4096
@@ -34,7 +38,7 @@
     return jnp.stack([real_part, imag_part]) / WIN
 
 
-def body(traces, row_ids):
+def body_by_rows(traces, row_ids):
     block_rows, _, band_bins = traces.shape
     trace_rows = traces.reshape(block_rows, 2 * band_bins)
     n_devices = lax.axis_size("chan")
@@ -82,6 +86,207 @@
     return jnp.stack(spectra_list, axis=2)
 
 
+LANES = 128
+CH = 8
+SLOTS = 2 * H + 1
+MESH = pl.DeviceIdType.MESH
+
+
+def exchange_kernel(n, xs_ref, pos_ref, o_ref, recv, placed, tmp, out, in_send, in_recv, out_send, out_recv):
+    me = lax.axis_index("chan")
+    rows = xs_ref.shape[1]
+
+    barrier = pltpu.get_barrier_semaphore()
+    for t in range(1, n):
+        pl.semaphore_signal(
+            barrier, inc=1, device_id={"chan": lax.rem(me + t, n)}, device_id_type=MESH
+        )
+    pl.semaphore_wait(barrier, n - 1)
+
+    def row_copy(t):
+        target = lax.rem(me + t, n)
+        return pltpu.make_async_remote_copy(
+            src_ref=xs_ref.at[target],
+            dst_ref=recv.at[t],
+            send_sem=in_send.at[t],
+            recv_sem=in_recv.at[t],
+            device_id={"chan": target},
+            device_id_type=MESH,
+        )
+
+    order = sorted(range(1, n), key=lambda t: -min(t, n - t))
+    for t in order:
+        row_copy(t).start()
+
+    def place(values, source, first):
+        pos = pos_ref[pl.ds(source, 1), :]
+
+        def chunk(b, carry):
+            target = lax.broadcasted_iota(jnp.int32, (rows, rows), 0) + b * rows
+            hot = jnp.where(pos == target, 1.0, 0.0).astype(jnp.bfloat16)
+            part = jnp.dot(hot, values, preferred_element_type=jnp.float32)
+            where = pl.ds(pl.multiple_of(b * rows, rows), rows)
+            if first:
+                placed[0, where, :] = part[:, :LANES]
+                placed[1, where, :] = part[:, LANES:]
+            else:
+                placed[0, where, :] += part[:, :LANES]
+                placed[1, where, :] += part[:, LANES:]
+            return carry
+
+        lax.fori_loop(0, n, chunk, 0)
+
+    place(xs_ref[me], me, True)
+    for t in reversed(order):
+        row_copy(t).wait_recv()
+        place(recv[t], lax.rem(me + n - t, n), False)
+
+    def result_copy(dest, k):
+        return pltpu.make_async_remote_copy(
+            src_ref=out.at[dest, k],
+            dst_ref=o_ref.at[me, k],
+            send_sem=out_send.at[dest, k],
+            recv_sem=out_recv.at[me, k],
+            device_id={"chan": dest},
+            device_id_type=MESH,
+        )
+
+    def deliver(dest, k):
+        @pl.when(dest != me)
+        def _():
+            result_copy(dest, k).start()
+
+        @pl.when(dest == me)
+        def _():
+            o_ref[me, k] = out[dest, k]
+
+    def pair(d, offset):
+        e = d + offset
+
+        def window(w, acc):
+            first = d * rows + w * CH
+            second = pl.ds(pl.multiple_of(e * rows + w * CH, CH), CH)
+            yr = placed[0, second, :]
+            yi = placed[1, second, :]
+            new = []
+            for c in range(CH):
+                xr = placed[0, pl.ds(first + c, 1), :]
+                xi = placed[1, pl.ds(first + c, 1), :]
+                re, im = acc[2 * c], acc[2 * c + 1]
+                new.append(re + (xr * yr + xi * yi))
+                new.append(im + (xi * yr - xr * yi))
+            return tuple(new)
+
+        zero = jnp.zeros((CH, LANES), jnp.float32)
+        acc = lax.fori_loop(0, WIN, window, (zero,) * (2 * CH), unroll=4)
+        for part in range(2):
+            for c in range(CH):
+                tmp[part, pl.ds(c * CH, CH), :] = acc[2 * c + part] * (1.0 / WIN)
+        for part in range(2):
+            out[d, H + offset, part] = tmp[part].astype(jnp.bfloat16)
+        deliver(d, H + offset)
+        if offset:
+            for part in range(2):
+                turned = jnp.concatenate(
+                    [tmp[part, pl.ds(c, CH, stride=CH), :] for c in range(CH)], axis=0
+                )
+                turned = turned if part == 0 else -turned
+                out[e, H - offset, part] = turned.astype(jnp.bfloat16)
+            deliver(e, H - offset)
+
+    def block_step(t, carry):
+        d = lax.rem(me + n // 2 + t, n)
+        pair(d, 0)
+        for offset in range(1, H + 1):
+            pl.when(d + offset < n)(functools.partial(pair, d, offset))
+        return carry
+
+    lax.fori_loop(0, n, block_step, 0)
+
+    for k in range(SLOTS):
+        partner = me + k - H
+
+        @pl.when((partner < 0) | (partner >= n))
+        def _():
+            for source in range(n):
+                o_ref[source, k] = jnp.zeros(o_ref.shape[2:], o_ref.dtype)
+
+    for t in range(1, n):
+        row_copy(t).wait_send()
+        dest = lax.rem(me + t, n)
+        source = lax.rem(me + n - t, n)
+        for k in range(SLOTS):
+            there = dest + k - H
+            here = me + k - H
+
+            @pl.when((there >= 0) & (there < n))
+            def _():
+                result_copy(dest, k).wait_send()
+
+            @pl.when((here >= 0) & (here < n))
+            def _():
+                pltpu.make_async_remote_copy(
+                    src_ref=out.at[source, k],
+                    dst_ref=o_ref.at[source, k],
+                    send_sem=out_send.at[source, k],
+                    recv_sem=out_recv.at[source, k],
+                    device_id={"chan": source},
+                    device_id_type=MESH,
+                ).wait_recv()
+
+
+def unpack_kernel(n, in_ref, out_ref):
+    for source in range(n):
+        for k in range(SLOTS):
+            values = in_ref[source, k, 0].astype(jnp.float32)
+            for c in range(CH):
+                out_ref[0, c, k, :, source * LANES : (source + 1) * LANES] = values[c * CH : (c + 1) * CH]
+
+
+def body_by_bins(traces, row_ids):
+    rows, _, band_bins = traces.shape
+    n = lax.axis_size("chan")
+    flat = traces.reshape(rows, 2 * band_bins)
+    white = scale_rows(flat, lax.psum(row_power(flat), "band"))
+    xs = white.reshape(rows, 2, n, LANES).transpose(2, 0, 1, 3).reshape(n, rows, 2 * LANES)
+    ids = lax.all_gather(row_ids, "chan")
+    pos = (ids // rows) * rows + (ids % WIN) * CH + (ids // WIN) % CH
+    vmem = pl.BlockSpec(memory_space=pltpu.VMEM)
+    packed = pl.pallas_call(
+        functools.partial(exchange_kernel, n),
+        out_shape=jax.ShapeDtypeStruct((n, SLOTS, 2, CH * CH, LANES), jnp.bfloat16),
+        in_specs=[vmem, vmem],
+        out_specs=vmem,
+        scratch_shapes=[
+            pltpu.VMEM((n, rows, 2 * LANES), jnp.bfloat16),
+            pltpu.VMEM((2, n * rows, LANES), jnp.float32),
+            pltpu.VMEM((2, CH * CH, LANES), jnp.float32),
+            pltpu.VMEM((n, SLOTS, 2, CH * CH, LANES), jnp.bfloat16),
+            pltpu.SemaphoreType.DMA((n,)),
+            pltpu.SemaphoreType.DMA((n,)),
+            pltpu.SemaphoreType.DMA((n, SLOTS)),
+            pltpu.SemaphoreType.DMA((n, SLOTS)),
+        ],
+        compiler_params=pltpu.CompilerParams(
+            collective_id=0, has_side_effects=True, vmem_limit_bytes=40 * 2**20
+        ),
+    )(xs, pos)
+    return pl.pallas_call(
+        functools.partial(unpack_kernel, n),
+        grid=(2,),
+        out_shape=jax.ShapeDtypeStruct((2, rows // WIN, SLOTS, CH, band_bins), jnp.float32),
+        in_specs=[pl.BlockSpec((n, SLOTS, 1, CH * CH, LANES), lambda p: (0, 0, p, 0, 0))],
+        out_specs=pl.BlockSpec((1, rows // WIN, SLOTS, CH, band_bins), lambda p: (p, 0, 0, 0, 0)),
+        compiler_params=pltpu.CompilerParams(vmem_limit_bytes=40 * 2**20),
+    )(packed)
+
+
+def body(traces, row_ids):
+    rows, _, band_bins = traces.shape
+    by_bins = band_bins == lax.axis_size("chan") * LANES and rows == CH * WIN
+    return (body_by_bins if by_bins else body_by_rows)(traces, row_ids)
+
+
 def solution(mesh):
     in_specs = (P("chan", None, "band"), P("chan"))
     out_specs = P(None, "chan", None, None, "band")

time: 210 us -> 88.4 us (0.42)
  waiting for transfers between devices: 116 us -> 0 us
  Pallas kernels: 0 us -> 58.4 us
  other arithmetic: 36.1 us -> 3.39 us
  starting transfers between devices: 25.9 us -> 0 us
  local copies, waits for them, and re-layouts: 20.7 us -> 3.16 us
  blocking collectives: 5.89 us -> 22.1 us
  matrix products: 4.15 us -> 0 us
    ppermute x4 -> x0, waiting for transfers between devices: 71.2 us -> none  [passed_along(): return lax.ppermute(block, axis, route)]
    pallas_call x0 -> x2, Pallas kernels: none -> 58.4 us  [the longest x1 56.6 us: body_by_bins(): pl.pallas_call(functools.partial(exchange_kernel, n), out_shape=jax.Shape...]
    all_to_all x2 -> x0, waiting for transfers between devices: 45.1 us -> none  [the longest x1 45.1 us: body(): lax.all_to_all(outgoing, 'chan', split_axis=0, concat_axis=0, tiled=True)]
    reduce_sum x2 -> x0, other arithmetic: 19.8 us -> none  [the longest x1 19.7 us: spectra_pair(): jnp.sum(first_real * second_real + first_imag * second_imag, axis=2)]
    all_gather x0 -> x1, blocking collectives: none -> 16.2 us  [body_by_bins(): ids = lax.all_gather(row_ids, 'chan')]
    ppermute x4 -> x0, starting transfers between devices: 13.8 us -> none  [passed_along(): return lax.ppermute(block, axis, route)]
    all_to_all x2 -> x0, starting transfers between devices: 12 us -> none  [the longest x1 6.05 us: body(): lax.all_to_all(sent_labels, 'chan', split_axis=0, concat_axis=0, tiled=True)]
    convert_element_type x8 -> x0, other arithmetic: 11.7 us -> none  [the longest x4 9.06 us: spectra_pair(): second_real = second[None, :, :, 0].astype(jnp.float32)]
  transfers between devices with their start and end apart: 6 -> 0, of which waited for: 3 -> 0; matrix products, arithmetic and copies ran while one was open for 14% -> 0% of each run, Pallas kernels for 0% -> 0%
where the time goes in v1:
time: 88.4 us; the launch traced here: 87.1 us
  Pallas kernels  58.4 us (66%)
  blocking collectives  22.1 us (25%)
  other arithmetic  3.39 us (4%)
  local copies, waits for them, and re-layouts  3.16 us (4%)
    pallas_call x1, Pallas kernels, body_by_bins(): pl.pallas_call(functools.partial(exchange_kernel, n), out_shape=jax.Shape...  56.6 us
    all_gather x1, blocking collectives, body_by_bins(): ids = lax.all_gather(row_ids, 'chan')  16.2 us
    psum x1, blocking collectives, body_by_bins(): white = scale_rows(flat, lax.psum(row_power(flat), 'band'))  5.89 us
    reduce_sum x1, other arithmetic, row_power(): return jnp.sum(values * values, axis=1)  3.02 us

profile of v1, /device:TPU:26, one launch (start us, length us, event | category | flops | bytes accessed | tf_op | source)
XLA Modules:
  0.0 87.1 jit_solution(2080778453203857224)
XLA Ops:
  0.0 3.0 %multiply_reduce_fusion = f32[256]{0:T(256)S(1)} fusion(bf16[256,2,1024]{2,1,0:T(2,128)(2,1)} %param.2), kind=kLoop, calls=%fused_computation.1 | loop fusion | flops 1572608 | bytes 1049600 | tf_op jit(solution)/shard_map/reduce_sum | solution.py:23
  3.0 5.9 %psum.7 = f32[256]{0:T(256)S(1)} all-reduce(f32[256]{0:T(256)S(1)} %multiply_reduce_fusion), channel_id=1, replica_groups=mesh['chan'=8,'band'=4] {'band'}, use_global_device_ids=true, to_apply=%region_1.0 | all-reduce | flops 256 | bytes 2048 | tf_op jit(solution)/shard_map/psum | solution.py:250
  8.9 16.2 %all-gather.1 = s32[8,1,256]{2,1,0:T(1,128)S(1)} all-gather(s32[1,1,256]{2,1,0:T(1,128)} %bitcast.25), channel_id=2, replica_groups=mesh['chan'=8,'band'=4] {'chan'}, dimensions={0}, use_global_device_ids=true | all-gather | bytes 9216 | tf_op jit(solution)/shard_map/all_gather | solution.py:252
  25.2 1.6 %reshape.15 = f32[256,2,8,128]{3,2,1,0:T(8,128)S(1)} reshape(bf16[256,2,1024]{2,1,0:T(2,128)(2,1)} %param.2) | data formatting | bytes 3145728 | tf_op jit(solution)/shard_map/convert_element_type | solution.py:28
  26.8 0.3 fusion
  27.2 0.8 copy.5
  28.0 0.7 reshape.14.xs_ref
  28.7 56.6 %shard_map.28.in_ref = bf16[8,5,2,64,128]{4,3,2,1,0:T(8,128)(2,1)S(1)} custom-call(bf16[8,256,256]{2,1,0:T(8,128)(2,1)S(1)} %reshape.14.xs_ref, s32[8,256]{1,0:T(8,128)S(1)} %fusion.4.pos_ref), custom_call_target="tpu_custom_call" | custom-call | tf_op jit(solution)/shard_map/pallas_call | solution.py:255
  85.3 1.8 %shard_map.29 = f32[2,8,5,8,1024]{4,3,2,1,0:T(8,128)} custom-call(bf16[8,5,2,64,128]{4,3,2,1,0:T(8,128)(2,1)S(1)} %shard_map.28.in_ref), custom_call_target="tpu_custom_call" | custom-call | tf_op jit(solution)/shard_map/pallas_call | solution.py:274
  (2 shorter events, 0.0 us)

commit v2 on v1

--- a/solution.py
+++ b/solution.py
@@ -92,54 +92,118 @@
 MESH = pl.DeviceIdType.MESH
 
 
-def exchange_kernel(n, xs_ref, pos_ref, o_ref, recv, placed, tmp, out, in_send, in_recv, out_send, out_recv):
+def exchange_kernel(
+    n, nb, flat_ref, pos_ref, o_ref, recv, placed, tmp, out, power, powers, label, labels,
+    in_send, in_recv, out_send, out_recv, power_send, power_recv, label_send, label_recv,
+):
     me = lax.axis_index("chan")
-    rows = xs_ref.shape[1]
+    mine = lax.axis_index("band")
+    rows, width = flat_ref.shape
+    band_bins = width // 2
 
     barrier = pltpu.get_barrier_semaphore()
     for t in range(1, n):
         pl.semaphore_signal(
             barrier, inc=1, device_id={"chan": lax.rem(me + t, n)}, device_id_type=MESH
         )
-    pl.semaphore_wait(barrier, n - 1)
-
-    def row_copy(t):
+    for t in range(1, nb):
+        pl.semaphore_signal(
+            barrier, inc=1, device_id={"band": lax.rem(mine + t, nb)}, device_id_type=MESH
+        )
+
+    total = jnp.zeros((rows, LANES), jnp.float32)
+    for i in range(width // LANES):
+        value = flat_ref[:, i * LANES : (i + 1) * LANES].astype(jnp.float32)
+        total += value * value
+    ones = jnp.ones((8, LANES), jnp.bfloat16)
+    row_sum = jnp.zeros((8, rows), jnp.float32)
+    for _ in range(3):
+        term = total.astype(jnp.bfloat16)
+        total -= term.astype(jnp.float32)
+        row_sum += lax.dot_general(
+            ones, term, (((1,), (1,)), ((), ())), preferred_element_type=jnp.float32
+        )
+    power[...] = row_sum
+
+    pl.semaphore_wait(barrier, n - 1 + nb - 1)
+
+    def power_copy(t):
+        return pltpu.make_async_remote_copy(
+            src_ref=power,
+            dst_ref=powers.at[t],
+            send_sem=power_send.at[t],
+            recv_sem=power_recv.at[t],
+            device_id={"band": lax.rem(mine + t, nb)},
+            device_id_type=MESH,
+        )
+
+    def label_copy(t):
+        return pltpu.make_async_remote_copy(
+            src_ref=label,
+            dst_ref=labels.at[t],
+            send_sem=label_send.at[t],
+            recv_sem=label_recv.at[t],
+            device_id={"chan": lax.rem(me + t, n)},
+            device_id_type=MESH,
+        )
+
+    def row_copy(t, part):
         target = lax.rem(me + t, n)
+        bins = pl.multiple_of(part * band_bins + target * LANES, LANES)
         return pltpu.make_async_remote_copy(
-            src_ref=xs_ref.at[target],
-            dst_ref=recv.at[t],
-            send_sem=in_send.at[t],
-            recv_sem=in_recv.at[t],
+            src_ref=flat_ref.at[:, pl.ds(bins, LANES)],
+            dst_ref=recv.at[t, part],
+            send_sem=in_send.at[t, part],
+            recv_sem=in_recv.at[t, part],
             device_id={"chan": target},
             device_id_type=MESH,
         )
 
+    for t in range(1, nb):
+        power_copy(t).start()
     order = sorted(range(1, n), key=lambda t: -min(t, n - t))
     for t in order:
-        row_copy(t).start()
-
-    def place(values, source, first):
-        pos = pos_ref[pl.ds(source, 1), :]
+        for part in range(2):
+            row_copy(t, part).start()
+
+    power_total = power[...]
+    for t in range(1, nb):
+        power_copy(t).wait_recv()
+        power_total += powers[t]
+    label[:8] = 1.0 / jnp.sqrt(power_total / F + 1e-06)
+    label[8:] = pos_ref[...].astype(jnp.float32)
+    for t in range(1, n):
+        label_copy(t).start()
+
+    def place(parts, held, first):
+        factor = jnp.transpose(held[:8])[:, :1]
+        pos = held[8:9].astype(jnp.int32)
+        values = jnp.concatenate(
+            [(x.astype(jnp.float32) * factor).astype(jnp.bfloat16) for x in parts], axis=1
+        )
 
         def chunk(b, carry):
             target = lax.broadcasted_iota(jnp.int32, (rows, rows), 0) + b * rows
             hot = jnp.where(pos == target, 1.0, 0.0).astype(jnp.bfloat16)
-            part = jnp.dot(hot, values, preferred_element_type=jnp.float32)
+            product = jnp.dot(hot, values, preferred_element_type=jnp.float32)
             where = pl.ds(pl.multiple_of(b * rows, rows), rows)
-            if first:
-                placed[0, where, :] = part[:, :LANES]
-                placed[1, where, :] = part[:, LANES:]
-            else:
-                placed[0, where, :] += part[:, :LANES]
-                placed[1, where, :] += part[:, LANES:]
+            for part in range(2):
+                term = product[:, part * LANES : (part + 1) * LANES]
+                placed[part, where, :] = term if first else placed[part, where, :] + term
             return carry
 
         lax.fori_loop(0, n, chunk, 0)
 
-    place(xs_ref[me], me, True)
+    own = [
+        flat_ref[:, pl.ds(pl.multiple_of(part * band_bins + me * LANES, LANES), LANES)]
+        for part in range(2)
+    ]
+    place(own, label[...], True)
     for t in reversed(order):
-        row_copy(t).wait_recv()
-        place(recv[t], lax.rem(me + n - t, n), False)
+        label_copy(t).wait_recv()
+        for part in range(2):
+            row_copy(t, part).wait_recv()
+        place([recv[t, 0], recv[t, 1]], labels[t], False)
 
     def result_copy(dest, k):
         return pltpu.make_async_remote_copy(
@@ -211,8 +275,12 @@
             for source in range(n):
                 o_ref[source, k] = jnp.zeros(o_ref.shape[2:], o_ref.dtype)
 
+    for t in range(1, nb):
+        power_copy(t).wait_send()
     for t in range(1, n):
-        row_copy(t).wait_send()
+        label_copy(t).wait_send()
+        for part in range(2):
+            row_copy(t, part).wait_send()
         dest = lax.rem(me + t, n)
         source = lax.rem(me + n - t, n)
         for k in range(SLOTS):
@@ -246,31 +314,38 @@
 def body_by_bins(traces, row_ids):
     rows, _, band_bins = traces.shape
     n = lax.axis_size("chan")
+    nb = lax.axis_size("band")
     flat = traces.reshape(rows, 2 * band_bins)
-    white = scale_rows(flat, lax.psum(row_power(flat), "band"))
-    xs = white.reshape(rows, 2, n, LANES).transpose(2, 0, 1, 3).reshape(n, rows, 2 * LANES)
-    ids = lax.all_gather(row_ids, "chan")
-    pos = (ids // rows) * rows + (ids % WIN) * CH + (ids // WIN) % CH
+    pos = (row_ids // rows) * rows + (row_ids % WIN) * CH + (row_ids // WIN) % CH
+    pos = jnp.broadcast_to(pos[None, :], (8, rows))
     vmem = pl.BlockSpec(memory_space=pltpu.VMEM)
     packed = pl.pallas_call(
-        functools.partial(exchange_kernel, n),
+        functools.partial(exchange_kernel, n, nb),
         out_shape=jax.ShapeDtypeStruct((n, SLOTS, 2, CH * CH, LANES), jnp.bfloat16),
         in_specs=[vmem, vmem],
         out_specs=vmem,
         scratch_shapes=[
-            pltpu.VMEM((n, rows, 2 * LANES), jnp.bfloat16),
+            pltpu.VMEM((n, 2, rows, LANES), jnp.bfloat16),
             pltpu.VMEM((2, n * rows, LANES), jnp.float32),
             pltpu.VMEM((2, CH * CH, LANES), jnp.float32),
             pltpu.VMEM((n, SLOTS, 2, CH * CH, LANES), jnp.bfloat16),
+            pltpu.VMEM((8, rows), jnp.float32),
+            pltpu.VMEM((nb, 8, rows), jnp.float32),
+            pltpu.VMEM((16, rows), jnp.float32),
+            pltpu.VMEM((n, 16, rows), jnp.float32),
+            pltpu.SemaphoreType.DMA((n, 2)),
+            pltpu.SemaphoreType.DMA((n, 2)),
+            pltpu.SemaphoreType.DMA((n, SLOTS)),
+            pltpu.SemaphoreType.DMA((n, SLOTS)),
+            pltpu.SemaphoreType.DMA((nb,)),
+            pltpu.SemaphoreType.DMA((nb,)),
             pltpu.SemaphoreType.DMA((n,)),
             pltpu.SemaphoreType.DMA((n,)),
-            pltpu.SemaphoreType.DMA((n, SLOTS)),
-            pltpu.SemaphoreType.DMA((n, SLOTS)),
         ],
         compiler_params=pltpu.CompilerParams(
             collective_id=0, has_side_effects=True, vmem_limit_bytes=40 * 2**20
         ),
-    )(xs, pos)
+    )(flat, pos)
     return pl.pallas_call(
         functools.partial(unpack_kernel, n),
         grid=(2,),

time: 88.4 us -> 70.8 us (0.80)
  blocking collectives: 22.1 us -> 0 us
  Pallas kernels: 58.4 us -> 67.6 us
  other arithmetic: 3.39 us -> 0.7 us
  local copies, waits for them, and re-layouts: 3.16 us -> 1.5 us
    all_gather x1 -> x0, blocking collectives: 16.2 us -> none  [body_by_bins(): ids = lax.all_gather(row_ids, 'chan')]
    pallas_call x1, Pallas kernels: 56.6 us -> 65.9 us  [body_by_bins(): pl.pallas_call(functools.partial(exchange_kernel, n, nb), out_shape=jax.S...]
    psum x1 -> x0, blocking collectives: 5.89 us -> none  [body_by_bins(): white = scale_rows(flat, lax.psum(row_power(flat), 'band'))]
    reduce_sum x1 -> x0, other arithmetic: 3.02 us -> none  [row_power(): return jnp.sum(values * values, axis=1)]
    convert_element_type x1 -> x0, local copies, waits for them, and re-layouts: 1.64 us -> none  [scale_rows(): trace_rows.astype(jnp.float32) * factor[:, None]]
    unnamed x0 -> x1, local copies, waits for them, and re-layouts: none -> 1.49 us
where the time goes in v2:
time: 70.8 us; the launch traced here: 69.8 us
  Pallas kernels  67.6 us (95%)
  local copies, waits for them, and re-layouts  1.5 us (2%)
    pallas_call x1, Pallas kernels, body_by_bins(): pl.pallas_call(functools.partial(exchange_kernel, n, nb), out_shape=jax.S...  65.9 us
    pallas_call x1, Pallas kernels, body_by_bins(): pl.pallas_call(functools.partial(unpack_kernel, n), grid=(2,), out_shape=...  1.77 us
    unnamed x1, local copies, waits for them, and re-layouts  1.49 us

profile of v2, /device:TPU:26, one launch (start us, length us, event | category | flops | bytes accessed | tf_op | source)
XLA Modules:
  0.0 69.8 jit_solution(10611720995249619357)
XLA Ops:
  0.0 0.7 fusion
  0.7 1.5 %copy.3 = bf16[32,8,2,1024]{3,1,2,0:T(8,128)(2,1)S(1)} copy(bf16[32,8,2,1024]{3,2,1,0:T(2,128)(2,1)} %bitcast.3) | data formatting | bytes 2097152
  2.2 65.9 %shard_map.28.in_ref = bf16[8,5,2,64,128]{4,3,2,1,0:T(8,128)(2,1)S(1)} custom-call(bf16[256,2048]{1,0:T(8,128)(2,1)S(1)} %bitcast.2, s32[8,256]{1,0:T(8,128)S(1)} %broadcast_in_dim.2.pos_ref), custom_call_target="tpu_custom_call" | custom-call | tf_op jit(solution)/shard_map/pallas_call | solution.py:322
  68.1 1.8 %shard_map.29 = f32[2,8,5,8,1024]{4,3,2,1,0:T(8,128)} custom-call(bf16[8,5,2,64,128]{4,3,2,1,0:T(8,128)(2,1)S(1)} %shard_map.28.in_ref), custom_call_target="tpu_custom_call" | custom-call | tf_op jit(solution)/shard_map/pallas_call | solution.py:349
  (1 shorter events, 0.0 us)

commit v3 on v2

--- a/solution.py
+++ b/solution.py
@@ -93,7 +93,7 @@
 
 
 def exchange_kernel(
-    n, nb, flat_ref, pos_ref, o_ref, recv, placed, tmp, out, power, powers, label, labels,
+    n, nb, flat_ref, ids_ref, o_ref, recv, hot, white, placed, tmp, out, power, powers, labels,
     in_send, in_recv, out_send, out_recv, power_send, power_recv, label_send, label_recv,
 ):
     me = lax.axis_index("chan")
@@ -123,7 +123,12 @@
         row_sum += lax.dot_general(
             ones, term, (((1,), (1,)), ((), ())), preferred_element_type=jnp.float32
         )
-    power[...] = row_sum
+    ids = ids_ref[...]
+    inside = ids & (rows - 1)
+    pos = ids - inside + (ids & (WIN - 1)) * CH + lax.shift_right_logical(inside, WIN.bit_length() - 1)
+    pos = jnp.broadcast_to(pos, (8, rows)).astype(jnp.float32)
+    upper = lax.broadcasted_iota(jnp.int32, (8, rows), 0) < 4
+    labels[0] = jnp.where(upper, row_sum, pos)
 
     pl.semaphore_wait(barrier, n - 1 + nb - 1)
 
@@ -139,7 +144,7 @@
 
     def label_copy(t):
         return pltpu.make_async_remote_copy(
-            src_ref=label,
+            src_ref=labels.at[0],
             dst_ref=labels.at[t],
             send_sem=label_send.at[t],
             recv_sem=label_recv.at[t],
@@ -159,51 +164,65 @@
             device_id_type=MESH,
         )
 
+    order = sorted(range(1, n), key=lambda t: -min(t, n - t))
+    for t in order:
+        label_copy(t).start()
+    for t in order:
+        for part in range(2):
+            row_copy(t, part).start()
+
+    power[0:1] = labels[0, 0:1]
+    for t in reversed(order):
+        label_copy(t).wait_recv()
+        power[t : t + 1] = labels[t, 0:1]
     for t in range(1, nb):
         power_copy(t).start()
-    order = sorted(range(1, n), key=lambda t: -min(t, n - t))
-    for t in order:
-        for part in range(2):
-            row_copy(t, part).start()
+
+    def hot_chunk(b, carry):
+        target = lax.broadcasted_iota(jnp.int32, (rows, rows), 0) + b * rows
+        where = pl.ds(pl.multiple_of(b * rows, rows), rows)
+        for t in range(n):
+            place = labels[t, 4:5].astype(jnp.int32)
+            hot[where, t * rows : (t + 1) * rows] = jnp.where(
+                place == target, 1.0, 0.0
+            ).astype(jnp.bfloat16)
+        return carry
+
+    lax.fori_loop(0, n, hot_chunk, 0)
 
     power_total = power[...]
     for t in range(1, nb):
         power_copy(t).wait_recv()
         power_total += powers[t]
-    label[:8] = 1.0 / jnp.sqrt(power_total / F + 1e-06)
-    label[8:] = pos_ref[...].astype(jnp.float32)
-    for t in range(1, n):
-        label_copy(t).start()
-
-    def place(parts, held, first):
-        factor = jnp.transpose(held[:8])[:, :1]
-        pos = held[8:9].astype(jnp.int32)
-        values = jnp.concatenate(
-            [(x.astype(jnp.float32) * factor).astype(jnp.bfloat16) for x in parts], axis=1
-        )
-
-        def chunk(b, carry):
-            target = lax.broadcasted_iota(jnp.int32, (rows, rows), 0) + b * rows
-            hot = jnp.where(pos == target, 1.0, 0.0).astype(jnp.bfloat16)
-            product = jnp.dot(hot, values, preferred_element_type=jnp.float32)
-            where = pl.ds(pl.multiple_of(b * rows, rows), rows)
-            for part in range(2):
-                term = product[:, part * LANES : (part + 1) * LANES]
-                placed[part, where, :] = term if first else placed[part, where, :] + term
-            return carry
-
-        lax.fori_loop(0, n, chunk, 0)
-
-    own = [
-        flat_ref[:, pl.ds(pl.multiple_of(part * band_bins + me * LANES, LANES), LANES)]
-        for part in range(2)
-    ]
-    place(own, label[...], True)
+    factor = jnp.transpose(1.0 / jnp.sqrt(power_total / F + 1e-06))
+
+    def whiten(t, parts):
+        for part in range(2):
+            value = parts[part].astype(jnp.float32) * factor[:, t : t + 1]
+            white[t * rows : (t + 1) * rows, part * LANES : (part + 1) * LANES] = value.astype(
+                jnp.bfloat16
+            )
+
+    whiten(
+        0,
+        [
+            flat_ref[:, pl.ds(pl.multiple_of(part * band_bins + me * LANES, LANES), LANES)]
+            for part in range(2)
+        ],
+    )
     for t in reversed(order):
-        label_copy(t).wait_recv()
         for part in range(2):
             row_copy(t, part).wait_recv()
-        place([recv[t, 0], recv[t, 1]], labels[t], False)
+        whiten(t, [recv[t, 0], recv[t, 1]])
+
+    def place_chunk(b, carry):
+        where = pl.ds(pl.multiple_of(b * rows, rows), rows)
+        product = jnp.dot(hot[where, :], white[...], preferred_element_type=jnp.float32)
+        placed[0, where, :] = product[:, :LANES]
+        placed[1, where, :] = product[:, LANES:]
+        return carry
+
+    lax.fori_loop(0, n, place_chunk, 0)
 
     def result_copy(dest, k):
         return pltpu.make_async_remote_copy(
@@ -316,8 +335,6 @@
     n = lax.axis_size("chan")
     nb = lax.axis_size("band")
     flat = traces.reshape(rows, 2 * band_bins)
-    pos = (row_ids // rows) * rows + (row_ids % WIN) * CH + (row_ids // WIN) % CH
-    pos = jnp.broadcast_to(pos[None, :], (8, rows))
     vmem = pl.BlockSpec(memory_space=pltpu.VMEM)
     packed = pl.pallas_call(
         functools.partial(exchange_kernel, n, nb),
@@ -326,13 +343,14 @@
         out_specs=vmem,
         scratch_shapes=[
             pltpu.VMEM((n, 2, rows, LANES), jnp.bfloat16),
+            pltpu.VMEM((n * rows, n * rows), jnp.bfloat16),
+            pltpu.VMEM((n * rows, 2 * LANES), jnp.bfloat16),
             pltpu.VMEM((2, n * rows, LANES), jnp.float32),
             pltpu.VMEM((2, CH * CH, LANES), jnp.float32),
             pltpu.VMEM((n, SLOTS, 2, CH * CH, LANES), jnp.bfloat16),
-            pltpu.VMEM((8, rows), jnp.float32),
-            pltpu.VMEM((nb, 8, rows), jnp.float32),
-            pltpu.VMEM((16, rows), jnp.float32),
-            pltpu.VMEM((n, 16, rows), jnp.float32),
+            pltpu.VMEM((n, rows), jnp.float32),
+            pltpu.VMEM((nb, n, rows), jnp.float32),
+            pltpu.VMEM((n, 8, rows), jnp.float32),
             pltpu.SemaphoreType.DMA((n, 2)),
             pltpu.SemaphoreType.DMA((n, 2)),
             pltpu.SemaphoreType.DMA((n, SLOTS)),
@@ -345,7 +363,7 @@
         compiler_params=pltpu.CompilerParams(
             collective_id=0, has_side_effects=True, vmem_limit_bytes=40 * 2**20
         ),
-    )(flat, pos)
+    )(flat, row_ids.reshape(1, rows))
     return pl.pallas_call(
         functools.partial(unpack_kernel, n),
         grid=(2,),

time: 70.8 us -> 62.7 us (0.89)
  the two profiles are of different devices: /device:TPU:26 before, /device:TPU:0 now
where the time goes in v3:
time: 62.7 us; the launch traced here: 62.5 us
  Pallas kernels  60.3 us (96%)
  local copies, waits for them, and re-layouts  2.16 us (3%)
    pallas_call x1, Pallas kernels, body_by_bins(): pl.pallas_call(functools.partial(exchange_kernel, n, nb), out_shape=jax.S...  58.5 us
    unnamed x3, local copies, waits for them, and re-layouts  2.16 us
    pallas_call x1, Pallas kernels, body_by_bins(): pl.pallas_call(functools.partial(unpack_kernel, n), grid=(2,), out_shape=...  1.77 us

profile of v3, /device:TPU:0, one launch (start us, length us, event | category | flops | bytes accessed | tf_op | source)
XLA Modules:
  0.0 62.5 jit_solution(15312223862691809226)
XLA Ops:
  0.0 1.5 %copy.3 = bf16[32,8,2,1024]{3,1,2,0:T(8,128)(2,1)S(1)} copy(bf16[32,8,2,1024]{3,2,1,0:T(2,128)(2,1)} %bitcast.5) | data formatting | bytes 2097152
  1.5 0.0 copy-start
  1.5 0.7 %copy-done = s32[256]{0:T(256)S(1)} copy-done((s32[256]{0:T(256)S(1)}, s32[256]{0:T(256)}, u32[]{:S(2)}) %copy-start) | copy-done | bytes 1048
  2.2 58.5 %shard_map.28.in_ref = bf16[8,5,2,64,128]{4,3,2,1,0:T(8,128)(2,1)S(1)} custom-call(bf16[256,2048]{1,0:T(8,128)(2,1)S(1)} %bitcast.3, s32[1,256]{1,0:T(1,128)S(1)} %bitcast.4), custom_call_target="tpu_custom_call" | custom-call | tf_op jit(solution)/shard_map/pallas_call | solution.py:339
  60.7 1.8 %shard_map.29 = f32[2,8,5,8,1024]{4,3,2,1,0:T(8,128)} custom-call(bf16[8,5,2,64,128]{4,3,2,1,0:T(8,128)(2,1)S(1)} %shard_map.28.in_ref), custom_call_target="tpu_custom_call" | custom-call | tf_op jit(solution)/shard_map/pallas_call | solution.py:367
Async XLA Ops:
  1.5 0.7 %copy-start = (s32[256]{0:T(256)S(1)}, s32[256]{0:T(256)}, u32[]{:S(2)}) copy-start(s32[256]{0:T(256)} %param.3) | copy-start | bytes 3076

commit v4 on v3

--- a/solution.py
+++ b/solution.py
@@ -215,19 +215,21 @@
             row_copy(t, part).wait_recv()
         whiten(t, [recv[t, 0], recv[t, 1]])
 
-    def place_chunk(b, carry):
+    def place_chunk(b):
         where = pl.ds(pl.multiple_of(b * rows, rows), rows)
         product = jnp.dot(hot[where, :], white[...], preferred_element_type=jnp.float32)
         placed[0, where, :] = product[:, :LANES]
         placed[1, where, :] = product[:, LANES:]
-        return carry
-
-    lax.fori_loop(0, n, place_chunk, 0)
+
+    start = me + n // 2
+    for i in range(H):
+        place_chunk(lax.rem(start + i, n))
 
     def result_copy(dest, k):
+        parts = 1 if k == H else 2
         return pltpu.make_async_remote_copy(
-            src_ref=out.at[dest, k],
-            dst_ref=o_ref.at[me, k],
+            src_ref=out.at[dest, k, :parts],
+            dst_ref=o_ref.at[me, k, :parts],
             send_sem=out_send.at[dest, k],
             recv_sem=out_recv.at[me, k],
             device_id={"chan": dest},
@@ -241,7 +243,8 @@
 
         @pl.when(dest == me)
         def _():
-            o_ref[me, k] = out[dest, k]
+            parts = 1 if k == H else 2
+            o_ref[me, k, :parts] = out[dest, k, :parts]
 
     def pair(d, offset):
         e = d + offset
@@ -262,23 +265,31 @@
 
         zero = jnp.zeros((CH, LANES), jnp.float32)
         acc = lax.fori_loop(0, WIN, window, (zero,) * (2 * CH), unroll=4)
+        if offset == 0:
+            partner = lax.broadcasted_iota(jnp.int32, (CH, LANES), 0)
+            for c in range(CH):
+                kept = jnp.where(partner >= c, acc[2 * c], acc[2 * c + 1])
+                tmp[0, pl.ds(c * CH, CH), :] = kept * (1.0 / WIN)
+            out[d, H, 0] = tmp[0].astype(jnp.bfloat16)
+            deliver(d, H)
+            return
         for part in range(2):
             for c in range(CH):
                 tmp[part, pl.ds(c * CH, CH), :] = acc[2 * c + part] * (1.0 / WIN)
         for part in range(2):
             out[d, H + offset, part] = tmp[part].astype(jnp.bfloat16)
         deliver(d, H + offset)
-        if offset:
-            for part in range(2):
-                turned = jnp.concatenate(
-                    [tmp[part, pl.ds(c, CH, stride=CH), :] for c in range(CH)], axis=0
-                )
-                turned = turned if part == 0 else -turned
-                out[e, H - offset, part] = turned.astype(jnp.bfloat16)
-            deliver(e, H - offset)
+        for part in range(2):
+            turned = jnp.concatenate(
+                [tmp[part, pl.ds(c, CH, stride=CH), :] for c in range(CH)], axis=0
+            )
+            turned = turned if part == 0 else -turned
+            out[e, H - offset, part] = turned.astype(jnp.bfloat16)
+        deliver(e, H - offset)
 
     def block_step(t, carry):
-        d = lax.rem(me + n // 2 + t, n)
+        pl.when(t < n - H)(lambda: place_chunk(lax.rem(start + t + H, n)))
+        d = lax.rem(start + t, n)
         pair(d, 0)
         for offset in range(1, H + 1):
             pl.when(d + offset < n)(functools.partial(pair, d, offset))
@@ -312,9 +323,10 @@
 
             @pl.when((here >= 0) & (here < n))
             def _():
+                parts = 1 if k == H else 2
                 pltpu.make_async_remote_copy(
-                    src_ref=out.at[source, k],
-                    dst_ref=o_ref.at[source, k],
+                    src_ref=out.at[source, k, :parts],
+                    dst_ref=o_ref.at[source, k, :parts],
                     send_sem=out_send.at[source, k],
                     recv_sem=out_recv.at[source, k],
                     device_id={"chan": source},
@@ -322,12 +334,24 @@
                 ).wait_recv()
 
 
-def unpack_kernel(n, in_ref, out_ref):
+def unpack_kernel(n, in_ref, out_ref, tmp):
+    part = pl.program_id(0)
+    partner = lax.broadcasted_iota(jnp.int32, (CH, LANES), 0)
     for source in range(n):
+        bins = slice(source * LANES, (source + 1) * LANES)
+        tmp[source] = in_ref[source, H, 0].astype(jnp.float32)
         for k in range(SLOTS):
-            values = in_ref[source, k, 0].astype(jnp.float32)
+            if k == H:
+                continue
+            values = in_ref[source, k, part].astype(jnp.float32)
             for c in range(CH):
-                out_ref[0, c, k, :, source * LANES : (source + 1) * LANES] = values[c * CH : (c + 1) * CH]
+                out_ref[0, c, k, :, bins] = values[c * CH : (c + 1) * CH]
+        for c in range(CH):
+            kept = tmp[source, pl.ds(c * CH, CH), :]
+            turned = tmp[source, pl.ds(c, CH, stride=CH), :]
+            real = jnp.where(partner >= c, kept, turned)
+            imag = jnp.where(partner < c, kept, jnp.where(partner > c, -turned, 0.0))
+            out_ref[0, c, H, :, bins] = jnp.where(part == 0, real, imag)
 
 
 def body_by_bins(traces, row_ids):
@@ -368,8 +392,9 @@
         functools.partial(unpack_kernel, n),
         grid=(2,),
         out_shape=jax.ShapeDtypeStruct((2, rows // WIN, SLOTS, CH, band_bins), jnp.float32),
-        in_specs=[pl.BlockSpec((n, SLOTS, 1, CH * CH, LANES), lambda p: (0, 0, p, 0, 0))],
+        in_specs=[pl.BlockSpec((n, SLOTS, 2, CH * CH, LANES), lambda p: (0, 0, 0, 0, 0))],
         out_specs=pl.BlockSpec((1, rows // WIN, SLOTS, CH, band_bins), lambda p: (p, 0, 0, 0, 0)),
+        scratch_shapes=[pltpu.VMEM((n, CH * CH, LANES), jnp.float32)],
         compiler_params=pltpu.CompilerParams(vmem_limit_bytes=40 * 2**20),
     )(packed)
 

time: 62.7 us -> 59 us (0.941)
  the two profiles are of different devices: /device:TPU:0 before, /device:TPU:26 now
where the time goes in v4:
time: 59 us; the launch traced here: 58.8 us
  Pallas kernels  56.7 us (96%)
  local copies, waits for them, and re-layouts  2.16 us (4%)
    pallas_call x1, Pallas kernels, body_by_bins(): pl.pallas_call(functools.partial(exchange_kernel, n, nb), out_shape=jax.S...  55 us
    unnamed x3, local copies, waits for them, and re-layouts  2.16 us
    pallas_call x1, Pallas kernels, body_by_bins(): pl.pallas_call(functools.partial(unpack_kernel, n), grid=(2,), out_shape=...  1.7 us

profile of v4, /device:TPU:26, one launch (start us, length us, event | category | flops | bytes accessed | tf_op | source)
XLA Modules:
  0.0 58.8 jit_solution(15033007340733900654)
XLA Ops:
  0.0 1.5 %copy.3 = bf16[32,8,2,1024]{3,1,2,0:T(8,128)(2,1)S(1)} copy(bf16[32,8,2,1024]{3,2,1,0:T(2,128)(2,1)} %bitcast.5) | data formatting | bytes 2097152
  1.5 0.0 copy-start
  1.5 0.7 %copy-done = s32[256]{0:T(256)S(1)} copy-done((s32[256]{0:T(256)S(1)}, s32[256]{0:T(256)}, u32[]{:S(2)}) %copy-start) | copy-done | bytes 1048
  2.2 55.0 %shard_map.28.in_ref = bf16[8,5,2,64,128]{4,3,2,1,0:T(8,128)(2,1)S(1)} custom-call(bf16[256,2048]{1,0:T(8,128)(2,1)S(1)} %bitcast.3, s32[1,256]{1,0:T(1,128)S(1)} %bitcast.4), custom_call_target="tpu_custom_call" | custom-call | tf_op jit(solution)/shard_map/pallas_call | solution.py:363
  57.1 1.7 %shard_map.29 = f32[2,8,5,8,1024]{4,3,2,1,0:T(8,128)} custom-call(bf16[8,5,2,64,128]{4,3,2,1,0:T(8,128)(2,1)S(1)} %shard_map.28.in_ref), custom_call_target="tpu_custom_call" | custom-call | tf_op jit(solution)/shard_map/pallas_call | solution.py:391
Async XLA Ops:
  1.5 0.7 %copy-start = (s32[256]{0:T(256)S(1)}, s32[256]{0:T(256)}, u32[]{:S(2)}) copy-start(s32[256]{0:T(256)} %param.3) | copy-start | bytes 3076

commit v5 on v4

--- a/solution.py
+++ b/solution.py
@@ -164,7 +164,7 @@
             device_id_type=MESH,
         )
 
-    order = sorted(range(1, n), key=lambda t: -min(t, n - t))
+    order = sorted(range(1, n), key=lambda t: min(t, n - t))
     for t in order:
         label_copy(t).start()
     for t in order:

time: 59 us -> 58.2 us (0.986); the launches traced: 58.8 us -> 57.3 us
  Pallas kernels: 56.7 us -> 55.1 us
    pallas_call x1, Pallas kernels: 55 us -> 53.4 us  [body_by_bins(): pl.pallas_call(functools.partial(exchange_kernel, n, nb), out_shape=jax.S...]
where the time goes in v5:
time: 58.2 us; the launch traced here: 57.3 us
  Pallas kernels  55.1 us (95%)
  local copies, waits for them, and re-layouts  2.16 us (4%)
    pallas_call x1, Pallas kernels, body_by_bins(): pl.pallas_call(functools.partial(exchange_kernel, n, nb), out_shape=jax.S...  53.4 us
    unnamed x3, local copies, waits for them, and re-layouts  2.16 us
    pallas_call x1, Pallas kernels, body_by_bins(): pl.pallas_call(functools.partial(unpack_kernel, n), grid=(2,), out_shape=...  1.7 us

profile of v5, /device:TPU:26, one launch (start us, length us, event | category | flops | bytes accessed | tf_op | source)
XLA Modules:
  0.0 57.3 jit_solution(7714575978679406796)
XLA Ops:
  0.0 1.5 %copy.3 = bf16[32,8,2,1024]{3,1,2,0:T(8,128)(2,1)S(1)} copy(bf16[32,8,2,1024]{3,2,1,0:T(2,128)(2,1)} %bitcast.5) | data formatting | bytes 2097152
  1.5 0.0 copy-start
  1.5 0.7 %copy-done = s32[256]{0:T(256)S(1)} copy-done((s32[256]{0:T(256)S(1)}, s32[256]{0:T(256)}, u32[]{:S(2)}) %copy-start) | copy-done | bytes 1048
  2.2 53.4 %shard_map.28.in_ref = bf16[8,5,2,64,128]{4,3,2,1,0:T(8,128)(2,1)S(1)} custom-call(bf16[256,2048]{1,0:T(8,128)(2,1)S(1)} %bitcast.3, s32[1,256]{1,0:T(1,128)S(1)} %bitcast.4), custom_call_target="tpu_custom_call" | custom-call | tf_op jit(solution)/shard_map/pallas_call | solution.py:363
  55.6 1.7 %shard_map.29 = f32[2,8,5,8,1024]{4,3,2,1,0:T(8,128)} custom-call(bf16[8,5,2,64,128]{4,3,2,1,0:T(8,128)(2,1)S(1)} %shard_map.28.in_ref), custom_call_target="tpu_custom_call" | custom-call | tf_op jit(solution)/shard_map/pallas_call | solution.py:391
Async XLA Ops:
  1.5 0.7 %copy-start = (s32[256]{0:T(256)S(1)}, s32[256]{0:T(256)}, u32[]{:S(2)}) copy-start(s32[256]{0:T(256)} %param.3) | copy-start | bytes 3076
